TPU v7x, 256 devices: a whole 4x4x8 slice. The times are simulated.
256 devices in a mesh: row: 16 (over y, z_lo), col: 16 (over z_hi, x, core).
Axes of the slice: x: 4, y: 4, z: 8 (z_hi: 2, z_lo: 4; z = z_hi * 4 + z_lo), core: 2. Of those that a mesh axis runs over, the one named last changes fastest.
Arguments:
- values: float32 [8192, 8192], P('row', 'col'), may hold values from 0.05 to 16
- tile_mask: int32 [32, 32], P('row', 'col'), may hold values from 0 to 1, as said below
Outputs:
- inflated: float32 [8192, 8192], P('row', 'col')
Inputs may be any that keep to these rules, and one draw needn't show every extreme that they name: `tile_mask`: every diagonal tile is 1; other tiles are 1 with a probability that differs by tile row and tile column.
All inputs are finite; a program needn't handle non-finite values.
Results may differ from a plain program's by a relative error of at most 0.00033.
Values may be sent and summed in bfloat16 or wider, within the bound.
A program may use at most 64 MiB of HBM per device.

v0:
```python
import jax
import jax.numpy as jnp
from jax import lax
from jax.experimental import pallas as pl
from jax.experimental.pallas import tpu as pltpu
from jax.sharding import PartitionSpec as P

TILE = 256
BLK = 512
HALF = BLK // 2
PARTS = 4
NBLK = 16
MESH = pl.DeviceIdType.MESH


def kernel(
    values_hbm,
    mask_hbm,
    scaled_ref,
    c_ref,
    a_buf,
    b_buf,
    masked,
    sums,
    send,
    z_recv,
    y_recv,
    x_recv,
    zh_recv,
    core_recv,
    far_recv,
    sum_send,
    sum_recv,
    values_ref,
    mask_ref,
    in_sem,
):
    r = lax.axis_index("row")
    c = lax.axis_index("col")
    y, zl = r // 4, r % 4
    zh, x, core = c // 8, (c // 2) % 4, c % 2
    middle = (zl + 1) // 2 == 1
    near = zl + 1 - 2 * (zl % 2)
    far_side = 3 - zl
    order = [zl, near, 2 - zl // 2, 3 - 3 * (zl // 2)]

    def at_y(d):
        return (((y + d) % 4) * 4 + zl, c)

    def at_zl(z):
        return (y * 4 + z, c)

    def at_x(d):
        return (r, zh * 8 + ((x + d) % 4) * 2 + core)

    across = (r, (c + 8) % 16)
    sibling = (r, c + 1 - 2 * core)

    values_in = [
        pltpu.make_async_copy(
            values_hbm.at[pl.ds(i * HALF, HALF)], values_ref.at[pl.ds(i * HALF, HALF)], in_sem.at[i]
        )
        for i in range(2)
    ]
    mask_in = pltpu.make_async_copy(mask_hbm, mask_ref, in_sem.at[2])
    mask_in.start()
    for cp in values_in:
        cp.start()

    barrier = pltpu.get_barrier_semaphore()
    shifts = [(dy, dz) for dy in range(4) for dz in range(4) if dy or dz]

    def in_column(dy, dz):
        return (((y + dy) % 4) * 4 + (zl + dz) % 4, c)

    partners = [in_column(dy, dz) for dy, dz in shifts]
    partners += [at_x(1), at_x(3), across, sibling]
    for p in partners:
        pl.semaphore_signal(barrier, inc=1, device_id=p, device_id_type=MESH)

    mask_in.wait()
    partial = []
    for i in range(2):
        values_in[i].wait()
        for j in range(2):
            rows, cols = pl.ds(i * TILE, TILE), pl.ds(j * TILE, TILE)
            masked[rows, cols] = values_ref[rows, cols] * mask_ref[i, j].astype(jnp.float32)
        partial.append(jnp.sum(masked[pl.ds(i * HALF, HALF)], axis=0, keepdims=True))
    sums[0, r] = partial[0] + partial[1]
    pl.semaphore_wait(barrier, len(partners))

    def sum_copy(base, n, slot):
        return pltpu.make_async_remote_copy(
            src_ref=sums.at[base, slot],
            dst_ref=sums.at[base, slot],
            send_sem=sum_send.at[base, n],
            recv_sem=sum_recv.at[base, n],
            device_id=in_column(*shifts[n]),
            device_id_type=MESH,
        )

    def start_sum(base):
        for n in range(len(shifts)):
            sum_copy(base, n, r).start()

    def finish_sum(base):
        for n, (dy, dz) in enumerate(shifts):
            sum_copy(base, n, ((y + 4 - dy) % 4) * 4 + (zl + 4 - dz) % 4).wait_recv()
        return jnp.sum(sums[base], axis=0)

    start_sum(0)
    c_ref[...] = jnp.zeros_like(c_ref)
    inverse = 1.0 / finish_sum(0)

    def make_stoch(h):
        rows = pl.ds(h * HALF, HALF)
        stoch = (masked[rows] * inverse).astype(jnp.bfloat16)
        b_buf[r, rows] = stoch
        a_buf[c, rows] = stoch


    pending = []
    inner = []

    def piece(buf, k, h):
        if h is None:
            return buf.at[k]
        n = PARTS if buf is a_buf else 2
        return buf.at[k, pl.ds(h * (BLK // n), BLK // n)]


    def push(buf, k, h, sem, dev):
        part = piece(buf, k, h)
        cp = pltpu.make_async_remote_copy(
            src_ref=part,
            dst_ref=part,
            send_sem=send.at[len(pending)],
            recv_sem=sem,
            device_id=dev,
            device_id_type=MESH,
        )
        cp.start()
        pending.append(cp)

    def take(buf, k, h, sem):
        part = piece(buf, k, h)
        pltpu.make_async_remote_copy(
            src_ref=part,
            dst_ref=part,
            send_sem=send.at[0],
            recv_sem=sem,
            device_id=sibling,
            device_id_type=MESH,
        ).wait_recv()

    def b_row(d, q):
        return ((y + d) % 4) * 4 + order[q]

    def a_col(s, d):
        return ((zh + s) % 2) * 8 + ((x + d) % 4) * 2 + core

    def z_start(h):
        push(b_buf, r, h, z_recv.at[zl, h], at_zl(near))
        if inner[-1]:
            push(b_buf, r, h, z_recv.at[zl, h], at_zl(far_side))

    def z_take(q, h):
        o = order[q]
        k = y * 4 + o
        take(b_buf, k, h, z_recv.at[o, h])
        if inner[-1]:
            push(b_buf, k, h, z_recv.at[o, h], at_zl(far_side if q == 1 else near))
        y_start(q, h)

    def y_start(q, h):
        k = b_row(0, q)
        push(b_buf, k, h, y_recv.at[0, q, h], at_y(1))
        push(b_buf, k, h, y_recv.at[1, q, h], at_y(3))

    def y_forward(q, h):
        k = b_row(3 if h == 0 else 1, q)
        take(b_buf, k, h, y_recv.at[h, q, h])
        push(b_buf, k, h, y_recv.at[2, q, h], at_y(1 if h == 0 else 3))

    def x_start(s, h):
        k = a_col(s, 0)
        push(a_buf, k, h, x_recv.at[s, 0, h], at_x(1))
        push(a_buf, k, h, x_recv.at[s, 1, h], at_x(3))

    def x_forward(s, h):
        d = 0 if h < PARTS // 2 else 1
        k = a_col(s, 3 if d == 0 else 1)
        take(a_buf, k, h, x_recv.at[s, d, h])
        push(a_buf, k, h, x_recv.at[s, 2, h], at_x(1 if d == 0 else 3))

    def to_sibling(s, d):
        push(a_buf, a_col(s, d), None, core_recv.at[s, d], sibling)

    def x_share(s):
        for h in range(PARTS // 2, PARTS):
            take(a_buf, a_col(s, 3), h, x_recv.at[s, 0, h])
        to_sibling(s, 3)
        for h in range(PARTS // 2):
            take(a_buf, a_col(s, 1), h, x_recv.at[s, 1, h])
        to_sibling(s, 1)

    def x_share_far(s):
        for h in range(PARTS):
            take(a_buf, a_col(s, 2), h, x_recv.at[s, 2, h])
            push(a_buf, a_col(s, 2), h, far_recv.at[s, h], sibling)

    def across_start(h):
        push(a_buf, c, h, zh_recv.at[h], across)

    def across_take(h):
        take(a_buf, a_col(1, 0), h, zh_recv.at[h])
        x_start(1, h)

    def rest(q):
        take(b_buf, b_row(3, q), 1, y_recv.at[0, q, 1])
        take(b_buf, b_row(1, q), 0, y_recv.at[1, q, 0])
        if q < 3:
            far(q)

    def far(q):
        for h in (0, 1):
            take(b_buf, b_row(2, q), h, y_recv.at[2, q, h])

    def from_sibling(s, d):
        k = ((zh + s) % 2) * 8 + ((x + d) % 4) * 2 + 1 - core
        if d == 2:
            for h in range(PARTS):
                take(a_buf, k, h, far_recv.at[s, h])
        else:
            take(a_buf, k, None, core_recv.at[s, d])

    def product(*ks):
        total = c_ref[...]
        for k in ks:
            total += jnp.dot(a_buf[k], b_buf[k], preferred_element_type=jnp.float32)
        c_ref[...] = total

    def products(q, s):
        k = ((zh + s) % 2) * 8 + order[q]
        product(k, k + 4)

    def a_late(k):
        return (k // 8 != zh) & ((k % 8) // 2 == (x + 2) % 4)

    def sweep_near():
        @pl.loop(0, NBLK // 2)
        def _(i):
            k = ((zh + 1) % 2) * 8 + i

            @pl.when(jnp.logical_not(a_late(k)) & (k % 4 != order[3]))
            def _():
                product(k)

    def sweep_fourth():
        for d in (0, 1, 3):
            k = b_row(d, 3)

            @pl.when(jnp.logical_not(a_late(k)))
            def _():
                product(k)

    def sweep_last():
        final = b_row(2, 3)
        for i in (0, 1):
            k = ((zh + 1) % 2) * 8 + ((x + 2) % 4) * 2 + i

            @pl.when(k != final)
            def _():
                product(k)

        far(3)
        product(final)

    def start_totals():
        sums[1, r] = jnp.sum(c_ref[...] * c_ref[...], axis=0, keepdims=True)
        start_sum(1)

    def wait_sent():
        for cp in pending:
            cp.wait_send()

    @pl.when(jnp.logical_not(middle))
    def _():
        inner.append(False)
        pending.clear()
        make_stoch(0)
        z_start(0)
        y_start(0, 0)
        make_stoch(1)
        z_start(1)
        y_start(0, 1)
        x_start(0, 0)
        x_start(0, 1)
        x_start(0, 2)
        x_start(0, 3)
        to_sibling(0, 0)
        z_take(1, 0)
        y_forward(0, 0)
        across_start(0)
        y_forward(0, 1)
        x_forward(0, 0)
        x_forward(0, 1)
        x_forward(0, 2)
        x_forward(0, 3)
        z_take(1, 1)
        across_start(1)
        y_forward(1, 0)
        x_share(0)
        z_take(2, 0)
        across_start(2)
        across_start(3)
        y_forward(1, 1)
        x_share_far(0)
        from_sibling(0, 0)
        from_sibling(0, 3)
        from_sibling(0, 1)
        from_sibling(0, 2)
        rest(0)
        products(0, 0)
        z_take(2, 1)
        across_take(0)
        y_forward(2, 0)
        across_take(1)
        z_take(3, 0)
        across_take(2)
        y_forward(2, 1)
        across_take(3)
        x_forward(1, 0)
        x_forward(1, 1)
        rest(1)
        products(1, 0)
        z_take(3, 1)
        x_forward(1, 2)
        x_forward(1, 3)
        to_sibling(1, 0)
        y_forward(3, 0)
        x_share(1)
        y_forward(3, 1)
        x_share_far(1)
        rest(2)
        products(2, 0)
        from_sibling(1, 0)
        from_sibling(1, 3)
        from_sibling(1, 1)
        sweep_near()
        rest(3)
        sweep_fourth()
        from_sibling(1, 2)
        sweep_last()
        start_totals()
        wait_sent()

    @pl.when(middle)
    def _():
        inner.append(True)
        pending.clear()
        make_stoch(0)
        z_start(0)
        y_start(0, 0)
        make_stoch(1)
        z_start(1)
        y_start(0, 1)
        x_start(0, 0)
        x_start(0, 1)
        x_start(0, 2)
        x_start(0, 3)
        to_sibling(0, 0)
        z_take(1, 0)
        z_take(2, 0)
        y_forward(0, 0)
        across_start(0)
        z_take(1, 1)
        z_take(2, 1)
        y_forward(0, 1)
        x_forward(0, 0)
        x_forward(0, 1)
        x_forward(0, 2)
        x_forward(0, 3)
        across_start(1)
        z_take(3, 0)
        y_forward(1, 0)
        x_share(0)
        z_take(3, 1)
        across_start(2)
        across_start(3)
        y_forward(1, 1)
        x_share_far(0)
        from_sibling(0, 0)
        from_sibling(0, 3)
        from_sibling(0, 1)
        from_sibling(0, 2)
        rest(0)
        products(0, 0)
        across_take(0)
        y_forward(2, 0)
        across_take(1)
        across_take(2)
        y_forward(2, 1)
        across_take(3)
        rest(1)
        products(1, 0)
        x_forward(1, 0)
        x_forward(1, 1)
        x_forward(1, 2)
        x_forward(1, 3)
        to_sibling(1, 0)
        y_forward(3, 0)
        x_share(1)
        y_forward(3, 1)
        x_share_far(1)
        rest(2)
        products(2, 0)
        from_sibling(1, 0)
        from_sibling(1, 3)
        from_sibling(1, 1)
        sweep_near()
        rest(3)
        sweep_fourth()
        from_sibling(1, 2)
        sweep_last()
        start_totals()
        wait_sent()

    scaled_ref[...] = c_ref[...] * jnp.sqrt(jnp.float32(BLK * NBLK) / finish_sum(1))
    for base in (0, 1):
        for n in range(len(shifts)):
            sum_copy(base, n, r).wait_send()


def shards(values, tile_mask):
    scaled = pl.pallas_call(
        kernel,
        out_shape=jax.ShapeDtypeStruct((BLK, BLK), jnp.float32),
        in_specs=[
            pl.BlockSpec(memory_space=pltpu.HBM),
            pl.BlockSpec(memory_space=pltpu.HBM),
        ],
        out_specs=pl.BlockSpec(memory_space=pltpu.VMEM),
        scratch_shapes=[
            pltpu.VMEM((BLK, BLK), jnp.float32),
            pltpu.VMEM((NBLK, BLK, BLK), jnp.bfloat16),
            pltpu.VMEM((NBLK, BLK, BLK), jnp.bfloat16),
            pltpu.VMEM((BLK, BLK), jnp.float32),
            pltpu.VMEM((2, NBLK, 1, BLK), jnp.float32),
            pltpu.SemaphoreType.DMA((110,)),
            pltpu.SemaphoreType.DMA((4, 2)),
            pltpu.SemaphoreType.DMA((3, 4, 2)),
            pltpu.SemaphoreType.DMA((2, 3, PARTS)),
            pltpu.SemaphoreType.DMA((PARTS,)),
            pltpu.SemaphoreType.DMA((2, 4)),
            pltpu.SemaphoreType.DMA((2, PARTS)),
            pltpu.SemaphoreType.DMA((2, 15)),
            pltpu.SemaphoreType.DMA((2, 15)),
            pltpu.VMEM((BLK, BLK), jnp.float32),
            pltpu.SMEM((2, 2), jnp.int32),
            pltpu.SemaphoreType.DMA((3,)),
        ],
        compiler_params=pltpu.CompilerParams(
            collective_id=0, has_side_effects=True, vmem_limit_bytes=52 * 2**20
        ),
        cost_estimate=pl.CostEstimate(
            flops=2 * BLK * BLK * BLK * NBLK, bytes_accessed=4 * 2**20, transcendentals=0
        ),
    )(values, tile_mask)
    return scaled * scaled


def solution(mesh):
    return jax.shard_map(
        shards,
        mesh=mesh,
        in_specs=(P("row", "col"), P("row", "col")),
        out_specs=P("row", "col"),
        check_vma=False,
    )
```

profile of v0, /device:TPU:2, one launch (start us, length us, event | category | flops | bytes accessed | tf_op | source)
XLA Modules:
  0.0 97.2 jit_solution(6261454177674522382)
XLA Ops:
  0.0 0.0 copy-start
  0.0 0.7 copy-done
  0.7 95.4 %shard_map.28 = f32[512,512]{1,0:T(8,128)S(1)} custom-call(f32[512,512]{1,0:T(8,128)} %values_hbm.1, s32[2,2]{1,0:T(2,128)S(1)} %copy-done), custom_call_target="tpu_custom_call" | custom-call | flops 4294967296 | bytes 4194304 | tf_op jit(solution)/shard_map/pallas_call | solution.py:436
  96.1 1.2 %mul.3 = f32[512,512]{1,0:T(8,128)} multiply(f32[512,512]{1,0:T(8,128)S(1)} %shard_map.28, f32[512,512]{1,0:T(8,128)S(1)} %shard_map.28) | non-fusion elementwise | flops 262144 | bytes 3145728 | tf_op jit(solution)/shard_map/mul | solution.py:470
Async XLA Ops:
  0.0 0.7 copy-start
where the time goes:
time: 97.4 us; the launch traced here: 97.2 us
  Pallas kernels  95.4 us (98%)
  other arithmetic  1.18 us (1%)
    pallas_call x1, Pallas kernels, shards(): pl.pallas_call(kernel, out_shape=jax.ShapeDtypeStruct((BLK, BLK), jnp.flo...  95.4 us

commit v1 on v0

--- a/solution.py
+++ b/solution.py
@@ -68,7 +68,7 @@
         cp.start()
 
     barrier = pltpu.get_barrier_semaphore()
-    shifts = [(dy, dz) for dy in range(4) for dz in range(4) if dy or dz]
+    shifts = [(dy, dz) for dy in (2, 1, 3, 0) for dz in (2, 3, 1, 0) if dy or dz]
 
     def in_column(dy, dz):
         return (((y + dy) % 4) * 4 + (zl + dz) % 4, c)
@@ -466,7 +466,10 @@
         cost_estimate=pl.CostEstimate(
             flops=2 * BLK * BLK * BLK * NBLK, bytes_accessed=4 * 2**20, transcendentals=0
         ),
-    )(values, tile_mask)
+    )(
+        pltpu.with_memory_space_constraint(values, pltpu.HBM),
+        pltpu.with_memory_space_constraint(tile_mask, pltpu.HBM),
+    )
     return scaled * scaled
 
 

time: 97.4 us -> 96.4 us (0.990)
  no operation moved by 1% of the time
where the time goes in v1:
time: 96.4 us; the launch traced here: 96.3 us
  Pallas kernels  95.2 us (99%)
  other arithmetic  1.18 us (1%)
    pallas_call x1, Pallas kernels, shards(): pl.pallas_call(kernel, out_shape=jax.ShapeDtypeStruct((BLK, BLK), jnp.flo...  95.2 us

profile of v1, /device:TPU:2, one launch (start us, length us, event | category | flops | bytes accessed | tf_op | source)
XLA Modules:
  0.0 96.3 jit_solution(11813289078730669196)
XLA Ops:
  0.0 95.2 %shard_map.28 = f32[512,512]{1,0:T(8,128)S(1)} custom-call(f32[512,512]{1,0:T(8,128)} %values_hbm.1, s32[2,2]{1,0:T(2,128)} %mask_hbm.1), custom_call_target="tpu_custom_call" | custom-call | flops 4294967296 | bytes 4194304 | tf_op jit(solution)/shard_map/pallas_call | solution.py:436
  95.2 1.2 %mul.3 = f32[512,512]{1,0:T(8,128)} multiply(f32[512,512]{1,0:T(8,128)S(1)} %shard_map.28, f32[512,512]{1,0:T(8,128)S(1)} %shard_map.28) | non-fusion elementwise | flops 262144 | bytes 3145728 | tf_op jit(solution)/shard_map/mul | solution.py:473

commit v2 on v1

--- a/solution.py
+++ b/solution.py
@@ -294,15 +294,15 @@
         make_stoch(1)
         z_start(1)
         y_start(0, 1)
+        z_take(1, 0)
+        y_forward(0, 0)
+        across_start(0)
+        y_forward(0, 1)
         x_start(0, 0)
         x_start(0, 1)
         x_start(0, 2)
         x_start(0, 3)
         to_sibling(0, 0)
-        z_take(1, 0)
-        y_forward(0, 0)
-        across_start(0)
-        y_forward(0, 1)
         x_forward(0, 0)
         x_forward(0, 1)
         x_forward(0, 2)
@@ -365,11 +365,6 @@
         make_stoch(1)
         z_start(1)
         y_start(0, 1)
-        x_start(0, 0)
-        x_start(0, 1)
-        x_start(0, 2)
-        x_start(0, 3)
-        to_sibling(0, 0)
         z_take(1, 0)
         z_take(2, 0)
         y_forward(0, 0)
@@ -377,6 +372,11 @@
         z_take(1, 1)
         z_take(2, 1)
         y_forward(0, 1)
+        x_start(0, 0)
+        x_start(0, 1)
+        x_start(0, 2)
+        x_start(0, 3)
+        to_sibling(0, 0)
         x_forward(0, 0)
         x_forward(0, 1)
         x_forward(0, 2)

time: 96.4 us -> 96.4 us (level)
  no operation moved by 1% of the time
where the time goes in v2:
time: 96.4 us; the launch traced here: 96.3 us
  Pallas kernels  95.2 us (99%)
  other arithmetic  1.18 us (1%)
    pallas_call x1, Pallas kernels, shards(): pl.pallas_call(kernel, out_shape=jax.ShapeDtypeStruct((BLK, BLK), jnp.flo...  95.2 us

profile of v2, /device:TPU:2, one launch (start us, length us, event | category | flops | bytes accessed | tf_op | source)
XLA Modules:
  0.0 96.3 jit_solution(15873719432123416887)
XLA Ops:
  0.0 95.2 %shard_map.28 = f32[512,512]{1,0:T(8,128)S(1)} custom-call(f32[512,512]{1,0:T(8,128)} %values_hbm.1, s32[2,2]{1,0:T(2,128)} %mask_hbm.1), custom_call_target="tpu_custom_call" | custom-call | flops 4294967296 | bytes 4194304 | tf_op jit(solution)/shard_map/pallas_call | solution.py:436
  95.2 1.2 %mul.3 = f32[512,512]{1,0:T(8,128)} multiply(f32[512,512]{1,0:T(8,128)S(1)} %shard_map.28, f32[512,512]{1,0:T(8,128)S(1)} %shard_map.28) | non-fusion elementwise | flops 262144 | bytes 3145728 | tf_op jit(solution)/shard_map/mul | solution.py:473
